TPU v7x, 32 devices: a whole 2x2x4 slice. The times are simulated.
32 devices in a mesh: ax: 4 (over y, x), az: 8 (over z, core).
Axes of the slice: x: 2, y: 2, z: 4, core: 2. Of those that a mesh axis runs over, the one named last changes fastest.
Arguments:
- saved_flow: float32 [3, 256, 64, 1024], P(None, 'az', None, 'ax'), may hold values from -6 to 6
- saved_adjoint: float32 [3, 256, 64, 1024], P(None, 'az', None, 'ax'), may hold values from -6 to 6
- tangent: float32 [3, 256, 64, 1024], P(None, 'az', None, 'ax'), may hold values from -6 to 6
- second_adjoint: float32 [3, 256, 64, 1024], P(None, 'az', None, 'ax'), may hold values from -6 to 6
- radial_rate: float32 [64], replicated, may hold values from 1 to 100
Outputs:
- tangent_next: float32 [3, 256, 64, 1024], P(None, 'az', None, 'ax')
- second_next: float32 [3, 256, 64, 1024], P(None, 'az', None, 'ax')
All inputs are finite; a program needn't handle non-finite values.
Results may differ from a plain program's by a relative error of at most 0.00005.
Values sent between devices are 32-bit elements; how exact they have to be, the bound alone decides.
A program may use at most 192 MiB of HBM per device.

v0:
```python
import math

import jax
import jax.numpy as jnp
from jax import lax
from jax.sharding import PartitionSpec as P

time_step = 0.1
viscosity = 0.005
axial_unit = 2.0 * math.pi / 20.0


def radial_table(count):
    points = jnp.arange(count, dtype=jnp.int32)[:, None]
    orders = jnp.arange(count, dtype=jnp.int32)[None, :]
    phases = orders * (2 * points + 1) % (4 * count)
    values = jnp.cos(phases.astype(jnp.float32) * (math.pi / (2.0 * count)))
    scales = jnp.where(orders == 0, math.sqrt(1.0 / count), math.sqrt(2.0 / count))
    return values * scales


def hartley_table(length):
    row_index = jnp.arange(length, dtype=jnp.int32)[:, None]
    col_index = jnp.arange(length, dtype=jnp.int32)[None, :]
    phases = row_index * col_index % length
    angles = phases.astype(jnp.float32) * (2.0 * math.pi / length)
    return (jnp.cos(angles) + jnp.sin(angles)) / math.sqrt(length)


def body(saved_flow, saved_adjoint, tangent, second_adjoint, radial_rate):
    components = tangent.shape[0]
    local_azimuth = tangent.shape[1]
    radial_count = tangent.shape[2]
    local_axial = tangent.shape[3]
    azimuth_count = local_azimuth * lax.axis_size("az")
    axial_count = local_axial * lax.axis_size("ax")
    radial = radial_table(radial_count)
    azimuth_table = hartley_table(azimuth_count)
    axial_table = hartley_table(axial_count)

    def along_azimuth(field):
        return jnp.einsum("nm,cmjk->cnjk", azimuth_table, field, precision=lax.Precision.HIGHEST)

    def along_axial(field):
        return jnp.einsum("nk,cmjk->cmjn", axial_table, field, precision=lax.Precision.HIGHEST)

    stacked = jnp.concatenate((saved_flow, saved_adjoint, tangent, second_adjoint), axis=0)
    grid = jnp.einsum("jr,cmrk->cmjk", radial, stacked, precision=lax.Precision.HIGHEST)
    halfway = along_azimuth(lax.all_to_all(grid, "az", split_axis=2, concat_axis=1, tiled=True))
    physical = along_axial(lax.all_to_all(halfway, "ax", split_axis=1, concat_axis=3, tiled=True))
    flow = physical[0:components]
    adjoint = physical[components : 2 * components]
    tang = physical[2 * components : 3 * components]
    second = physical[3 * components : 4 * components]
    flow_sum = jnp.sum(flow, axis=0)[None]
    adjoint_sum = jnp.sum(adjoint, axis=0)[None]
    tang_sum = jnp.sum(tang, axis=0)[None]
    second_sum = jnp.sum(second, axis=0)[None]
    tangent_rhs = flow * tang_sum + tang * flow_sum
    second_rhs = flow * second_sum + second * flow_sum + adjoint * tang_sum + tang * adjoint_sum
    products = jnp.concatenate((tangent_rhs, second_rhs), axis=0)
    partial_field = along_axial(products)
    turned = along_azimuth(
        lax.all_to_all(partial_field, "ax", split_axis=3, concat_axis=1, tiled=True)
    )
    spectral = jnp.einsum(
        "jr,cmjk->cmrk",
        radial,
        lax.all_to_all(turned, "az", split_axis=1, concat_axis=2, tiled=True),
        precision=lax.Precision.HIGHEST,
    )
    azimuth = lax.axis_index("az") * local_azimuth + jnp.arange(local_azimuth, dtype=jnp.int32)
    wave_azimuth = jnp.minimum(azimuth, azimuth_count - azimuth).astype(jnp.float32)
    axial = lax.axis_index("ax") * local_axial + jnp.arange(local_axial, dtype=jnp.int32)
    wave_axial = jnp.minimum(axial, axial_count - axial).astype(jnp.float32) * axial_unit
    total = (
        radial_rate[None, :, None]
        + (wave_azimuth**2)[:, None, None]
        + (wave_axial**2)[None, None, :]
    )
    denom = (1.0 + viscosity * total)[None]
    tangent_next = (tangent + time_step * spectral[0:components]) / denom
    second_next = (second_adjoint + time_step * spectral[components : 2 * components]) / denom
    return (tangent_next, second_next)


def solution(mesh):
    in_specs = (
        P(None, "az", None, "ax"),
        P(None, "az", None, "ax"),
        P(None, "az", None, "ax"),
        P(None, "az", None, "ax"),
        P(),
    )
    out_specs = (P(None, "az", None, "ax"), P(None, "az", None, "ax"))
    return jax.shard_map(body, mesh=mesh, in_specs=in_specs, out_specs=out_specs, check_vma=False)
```

profile of v0, /device:TPU:0, one launch (start us, length us, event | category | flops | bytes accessed | tf_op | source)
XLA Modules:
  0.0 1845.0 jit_solution(688436716861443825)
XLA Ops:
  0.7 0.0 copy-start.2
  0.7 29.4 %fusion.20 = f32[12,32,64,256]{3,2,1,0:T(8,128)} fusion(f32[3,32,64,256]{3,2,1,0:T(8,128)} %param.8, f32[3,32,64,256]{3,2,1,0:T(8,128)} %param.7, f32[3,32,64,256]{3,2,1,0:T(8,128)} %param.6, f32[3,32,64,256]{3,2,1,0:T(8,128)} %param.5, f32[64]{0:T(128)S(1)} %compare_select_fusion, s32[64]{0:T(128)S(1)} %multiply_add_fusion.3), kind=kOutput, calls=%fused_computation.18 | convolution fusion | flops 4850774016 | bytes 50332160 | tf_op jit(solution)/shard_map/jr,cmrk->cmjk/dot_general | solution.py:48
  30.1 21.8 %copy.48 = f32[12,32,64,256]{3,1,0,2:T(8,128)S(1)} copy(f32[12,32,64,256]{3,2,1,0:T(8,128)} %fusion.20) | data formatting | bytes 50331648 | tf_op jit(solution)/shard_map/jr,cmrk->cmjk/transpose | solution.py:48
  51.9 550.9 %all_to_all.72 = f32[12,32,64,256]{3,1,0,2:T(8,128)} all-to-all(f32[12,32,64,256]{3,1,0,2:T(8,128)S(1)} %copy.48), channel_id=1, replica_groups=mesh['ax'=4,'az'=8] {'az'}, dimensions={2} | all-to-all | bytes 50331648 | tf_op jit(solution)/shard_map/all_to_all | solution.py:49
  602.8 28.3 %copy.50 = f32[12,8,32,8,256]{4,3,2,1,0:T(8,128)} copy(f32[12,8,32,8,256]{4,2,0,3,1:T(8,128)} %bitcast.63) | data formatting | bytes 50331648 | tf_op jit(solution)/shard_map/all_to_all | solution.py:49
  631.1 56.0 %fusion.17 = f32[12,256,8,256]{1,3,2,0:T(8,128)} fusion(f32[12,256,8,256]{3,2,1,0:T(8,128)} %bitcast.62), kind=kOutput, calls=%fused_computation.17 | convolution fusion | flops 19328401408 | bytes 50331648 | tf_op jit(solution)/shard_map/nm,cmjk->cnjk/dot_general | solution.py:42
  687.2 25.1 %copy.52 = f32[12,256,8,256]{3,2,0,1:T(8,128)} copy(f32[12,256,8,256]{1,3,2,0:T(8,128)} %fusion.17) | data formatting | bytes 50331648 | tf_op jit(solution)/shard_map/nm,cmjk->cnjk/transpose | solution.py:42
  712.2 8.5 all-to-all-start.1
  720.7 17.7 fusion.118
  738.4 254.3 %all-to-all-done.1 = f32[12,256,8,256]{3,2,0,1:T(8,128)} async-done(((f32[12,256,8,256]{3,2,0,1:T(8,128)}), f32[12,256,8,256]{3,2,0,1:T(8,128)}, u32[]{:S(2)}, u32[]{:S(2)}) %all-to-all-start.1) | async-done | bytes 25165856 | tf_op jit(solution)/shard_map/all_to_all | solution.py:50
  992.7 10.4 copy.54
  1003.1 85.3 %fusion.34 = f32[12,64,8,1024]{3,2,1,0:T(8,128)} fusion(f32[12,64,8,1024]{3,2,1,0:T(8,128)S(1)} %bitcast.68, f32[1024,1024,1,1]{1,0,3,2:T(8,128)} %fusion.118), kind=kOutput, calls=%fused_computation.40 | convolution fusion | flops 77309411328 | bytes 54525952 | tf_op jit(solution)/shard_map/nk,cmjk->cmjn/dot_general | solution.py:45
  1088.4 12.1 slice_reduce_fusion.2
  1100.5 15.1 multiply_add_fusion.1
  1115.6 11.9 fusion.116
  1127.6 63.1 %fusion.10 = f32[6,64,8,1024]{3,2,1,0:T(8,128)} fusion(f32[6,64,8,1024]{3,2,1,0:T(8,128)} %fusion.116), kind=kOutput, calls=%fused_computation.10 | convolution fusion | flops 38671482880 | bytes 25165824 | tf_op jit(solution)/shard_map/nk,cmjk->cmjn/dot_general | solution.py:45
  1190.7 21.3 %copy.55 = f32[6,64,8,1024]{1,2,0,3:T(8,128)} copy(f32[6,64,8,1024]{3,2,1,0:T(8,128)} %fusion.10) | data formatting | bytes 25165824 | tf_op jit(solution)/shard_map/nk,cmjk->cmjn/dot_general | solution.py:45
  1212.0 33.5 %reshape.77 = f32[4,1,786432]{2,1,0:T(1,128)} reshape(f32[1024,6,8,64]{3,2,1,0:T(8,128)} %bitcast.64) | data formatting | bytes 25165824
  1245.5 146.5 %all_to_all.73 = f32[4,1,786432]{2,1,0:T(1,128)} all-to-all(f32[4,1,786432]{2,1,0:T(1,128)} %reshape.77), channel_id=1, replica_groups=mesh['ax'=4,'az'=8] {'ax'}, dimensions={0} | all-to-all | bytes 25165824 | tf_op jit(solution)/shard_map/all_to_all | solution.py:64
  1392.1 0.5 broadcast.144
  1392.6 39.8 %reduce = f32[4,786432]{1,0:T(4,128)} reduce(f32[4,1,786432]{2,1,0:T(1,128)} %all_to_all.73, f32[]{:T(128)} %broadcast.144), dimensions={1}, to_apply=%all_to_all.60.reduce_sub_computation | reduce | bytes 25165828 | tf_op jit(solution)/shard_map/all_to_all | solution.py:64
  1432.4 32.1 %reshape.78 = f32[1024,6,8,64]{3,2,1,0:T(8,128)} reshape(f32[4,786432]{1,0:T(4,128)} %reduce) | data formatting | bytes 25165824
  1464.5 20.3 %copy.69 = f32[6,64,8,4,256]{4,3,2,1,0:T(4,128)} copy(f32[6,64,8,4,256]{1,2,0,4,3:T(8,128)} %bitcast.65) | data formatting | bytes 25165824 | tf_op jit(solution)/shard_map/all_to_all | solution.py:64
  1484.8 16.3 copy.71
  1501.1 27.3 %convolution_bitcast_fusion = f32[6,256,8,256]{1,3,2,0:T(8,128)} fusion(f32[6,256,8,256]{3,1,2,0:T(8,128)} %bitcast.66), kind=kOutput, calls=%fused_computation.35 | convolution fusion | flops 9664724992 | bytes 25165824 | tf_op jit(solution)/shard_map/nm,cmjk->cnjk/dot_general | solution.py:42
  1528.4 12.8 copy.59
  1541.2 5.7 all-to-all-start.3
  1547.0 0.1 broadcast_add_fusion
  1547.0 0.3 multiply_add_fusion.2
  1547.4 273.3 %all-to-all-done.3 = f32[6,256,8,256]{3,2,0,1:T(8,128)} async-done(((f32[6,256,8,256]{3,2,0,1:T(8,128)}), f32[6,256,8,256]{3,2,0,1:T(8,128)}, u32[]{:S(2)}, u32[]{:S(2)}) %all-to-all-start.3) | async-done | bytes 12582944 | tf_op jit(solution)/shard_map/all_to_all | solution.py:69
  1820.7 15.0 fusion.27
  1835.7 9.1 fusion.24
  (13 shorter events, 0.0 us)
Async XLA Ops:
  0.6 29.5 %copy-start = (f32[64]{0:T(128)}, f32[64]{0:T(128)S(1)}, u32[]{:S(2)}) copy-start(f32[64]{0:T(128)S(1)} %compare_select_fusion) | copy-start | bytes 772
  0.7 29.4 %copy-start.2 = (s32[64]{0:T(128)}, s32[64]{0:T(128)S(1)}, u32[]{:S(2)}) copy-start(s32[64]{0:T(128)S(1)} %multiply_add_fusion.3) | copy-start | bytes 772
  712.2 280.5 %all-to-all-start.1 = ((f32[12,256,8,256]{3,2,0,1:T(8,128)}), f32[12,256,8,256]{3,2,0,1:T(8,128)}, u32[]{:S(2)}, u32[]{:S(2)}) async-start(f32[12,256,8,256]{3,2,0,1:T(8,128)} %copy.52), calls=%async_computation.1 | async-start | bytes 50331648 | tf_op jit(solution)/shard_map/all_to_all | solution.py:50
  1541.2 5.7 copy-start.4
  1541.2 279.5 %copy-start.1 = (f32[64]{0:T(128)S(1)}, f32[64]{0:T(128)}, u32[]{:S(2)}) copy-start(f32[64]{0:T(128)} %copy-done) | copy-start | bytes 772
  1541.2 279.5 %copy-start.3 = (s32[64]{0:T(128)S(1)}, s32[64]{0:T(128)}, u32[]{:S(2)}) copy-start(s32[64]{0:T(128)} %copy-done.2) | copy-start | bytes 772
  1541.2 279.5 %all-to-all-start.3 = ((f32[6,256,8,256]{3,2,0,1:T(8,128)}), f32[6,256,8,256]{3,2,0,1:T(8,128)}, u32[]{:S(2)}, u32[]{:S(2)}) async-start(f32[6,256,8,256]{3,2,0,1:T(8,128)} %copy.59), calls=%async_computation.3 | async-start | bytes 25165824 | tf_op jit(solution)/shard_map/all_to_all | solution.py:69
where the time goes:
time: 1850 us
  blocking collectives  697 us (38%)
  waiting for transfers between devices  528 us (29%)
  matrix products  276 us (15%)
  local copies, waits for them, and re-layouts  223 us (12%)
  other arithmetic  106 us (6%)
    all_to_all x1, blocking collectives, body(): lax.all_to_all(grid, 'az', split_axis=2, concat_axis=1, tiled=True)  551 us
    all_to_all x1, waiting for transfers between devices, body(): lax.all_to_all(turned, 'az', split_axis=1, concat_axis=2, tiled=True)  273 us
    all_to_all x1, waiting for transfers between devices, body(): lax.all_to_all(halfway, 'ax', split_axis=1, concat_axis=3, tiled=True)  254 us
    dot_general x2, matrix products, along_axial(): jnp.einsum('nk,cmjk->cmjn', axial_table, field, precision=lax.Precision.H...  148 us
    all_to_all x1, blocking collectives, body(): lax.all_to_all(partial_field, 'ax', split_axis=3, concat_axis=1, tiled=True)  147 us
    dot_general x2, matrix products, along_azimuth(): jnp.einsum('nm,cmjk->cnjk', azimuth_table, field, precision=lax.Precision...  83.3 us
    unnamed x12, local copies, waits for them, and re-layouts  65.7 us
    all_to_all x1, other arithmetic, body(): lax.all_to_all(partial_field, 'ax', split_axis=3, concat_axis=1, tiled=True)  39.8 us
  transfers between devices with their start and end apart: 2, of which 2 were waited for; matrix products, arithmetic and copies ran while one was open for 1% of the time, Pallas kernels for 0%

commit v1 on v0

v1 whole, which is shorter than its diff:
```python
import functools
import math

import jax
import jax.numpy as jnp
import ml_dtypes
import numpy as np
from jax import lax
from jax.experimental import pallas as pl
from jax.experimental.pallas import tpu as pltpu
from jax.sharding import PartitionSpec as P

time_step = 0.1
viscosity = 0.005
axial_unit = 2.0 * math.pi / 20.0
lookahead = 3
MESH = pl.DeviceIdType.MESH


def radial_table(count):
    points = np.arange(count)[:, None]
    orders = np.arange(count)[None, :]
    phases = orders * (2 * points + 1) % (4 * count)
    values = np.cos(phases * (math.pi / (2.0 * count)))
    scales = np.where(orders == 0, math.sqrt(1.0 / count), math.sqrt(2.0 / count))
    return values * scales


def hartley_table(length):
    phases = np.arange(length)[:, None] * np.arange(length)[None, :] % length
    angles = phases * (2.0 * math.pi / length)
    return (np.cos(angles) + np.sin(angles)) / math.sqrt(length)


def halves(table):
    high = table.astype(ml_dtypes.bfloat16)
    low = (table - high.astype(np.float64)).astype(ml_dtypes.bfloat16)
    return jnp.asarray(np.stack((high, low)))


def split(value):
    high = value.astype(jnp.bfloat16)
    low = (value - high.astype(jnp.float32)).astype(jnp.bfloat16)
    return high, low


def dot(left, right):
    return jnp.dot(left, right, preferred_element_type=jnp.float32)


def kernel(
    az,
    ax,
    grid_ref,
    azimuth_ref,
    axial_ref,
    out_ref,
    back_ref,
    columns,
    rows,
    high_rows,
    low_rows,
    send_in,
    recv_in,
    send_over,
    recv_over,
    send_back,
    recv_back,
    send_out,
    recv_out,
    own,
):
    steps, fields, azimuth_count, local_axial = columns.shape
    produced = out_ref.shape[1]
    local_azimuth = azimuth_count // az
    middle = azimuth_count // ax
    axial_count = rows.shape[3]
    group = high_rows.shape[0] // middle
    my_az = lax.axis_index("az")
    my_ax = lax.axis_index("ax")

    def az_rows(place):
        return pl.ds(pl.multiple_of(place * local_azimuth, local_azimuth), local_azimuth)

    def ax_rows(place):
        return pl.ds(pl.multiple_of(place * middle, middle), middle)

    def ax_lanes(place):
        return pl.ds(pl.multiple_of(place * local_axial, local_axial), local_axial)

    def copy_in(step, hop):
        target = (my_az + hop) % az
        return pltpu.make_async_remote_copy(
            src_ref=grid_ref.at[target * steps + step],
            dst_ref=columns.at[step, :, az_rows(my_az), :],
            send_sem=send_in.at[step, hop - 1],
            recv_sem=recv_in.at[step, hop - 1],
            device_id={"az": target},
            device_id_type=MESH,
        )

    def own_in(step):
        return pltpu.make_async_copy(
            grid_ref.at[my_az * steps + step],
            columns.at[step, :, az_rows(my_az), :],
            own.at[0, step],
        )

    def copy_over(step, hop):
        target = (my_ax + hop) % ax
        return pltpu.make_async_remote_copy(
            src_ref=columns.at[step, :, ax_rows(target), :],
            dst_ref=rows.at[step, :, :, ax_lanes(my_ax)],
            send_sem=send_over.at[step, hop - 1],
            recv_sem=recv_over.at[step, hop - 1],
            device_id={"ax": target},
            device_id_type=MESH,
        )

    def own_over(step):
        return pltpu.make_async_copy(
            columns.at[step, :, ax_rows(my_ax), :],
            rows.at[step, :, :, ax_lanes(my_ax)],
            own.at[1, step],
        )

    def copy_back(step, hop):
        target = (my_ax + hop) % ax
        return pltpu.make_async_remote_copy(
            src_ref=rows.at[step, pl.ds(0, produced), :, ax_lanes(target)],
            dst_ref=back_ref.at[step, :, ax_rows(my_ax), :],
            send_sem=send_back.at[step, hop - 1],
            recv_sem=recv_back.at[step, hop - 1],
            device_id={"ax": target},
            device_id_type=MESH,
        )

    def own_back(step):
        return pltpu.make_async_copy(
            rows.at[step, pl.ds(0, produced), :, ax_lanes(my_ax)],
            back_ref.at[step, :, ax_rows(my_ax), :],
            own.at[2, step],
        )

    def copy_out(step, hop):
        target = (my_az + hop) % az
        return pltpu.make_async_remote_copy(
            src_ref=columns.at[step, pl.ds(0, produced), az_rows(target), :],
            dst_ref=out_ref.at[my_az * steps + step],
            send_sem=send_out.at[step, hop - 1],
            recv_sem=recv_out.at[step, hop - 1],
            device_id={"az": target},
            device_id_type=MESH,
        )

    def own_out(step):
        return pltpu.make_async_copy(
            columns.at[step, pl.ds(0, produced), az_rows(my_az), :],
            out_ref.at[my_az * steps + step],
            own.at[3, step],
        )

    def start(count, copy, mine, step):
        def each(hop, carry):
            copy(step, hop).start()
            return carry

        lax.fori_loop(1, count, each, 0)
        mine(step).start()

    def arrive(count, copy, mine, step):
        def each(hop, carry):
            copy(step, hop).wait_recv()
            return carry

        mine(step).wait()
        lax.fori_loop(1, count, each, 0)

    def leave(count, copy, step):
        def each(hop, carry):
            copy(step, hop).wait_send()
            return carry

        lax.fori_loop(1, count, each, 0)

    def along_azimuth(step, count):
        def each(field, carry):
            high, low = split(columns[step, field])
            columns[step, field] = dot(azimuth_ref[0], high) + (
                dot(azimuth_ref[1], high) + dot(azimuth_ref[0], low)
            )
            return carry

        lax.fori_loop(0, count, each, 0)

    tile = min(256, axial_count)

    def along_axial(step, count):
        def each(part, carry):
            first = part * group

            def cast(place, carry):
                high, low = split(rows[step, first + place])
                at = pl.ds(pl.multiple_of(place * middle, middle), middle)
                high_rows[at, :] = high
                low_rows[at, :] = low
                return carry

            lax.fori_loop(0, group, cast, 0)

            def turn(place, carry):
                lanes = pl.ds(pl.multiple_of(place * tile, tile), tile)
                high = axial_ref[0, :, lanes]
                low = axial_ref[1, :, lanes]
                value = dot(high_rows[...], high) + (
                    dot(high_rows[...], low) + dot(low_rows[...], high)
                )
                rows[step, pl.ds(first, group), :, lanes] = value.reshape(group, middle, tile)
                return carry

            lax.fori_loop(0, axial_count // tile, turn, 0)
            return carry

        lax.fori_loop(0, count // group, each, 0)

    def multiply(step):
        components = fields // 4

        def each(place, carry):
            at = pl.ds(pl.multiple_of(place * 8, 8), 8)
            for first in range(0, axial_count, tile):
                lanes = pl.ds(first, tile)
                values = [rows[step, field, at, lanes] for field in range(fields)]
                flow = values[0:components]
                adjoint = values[components : 2 * components]
                tang = values[2 * components : 3 * components]
                second = values[3 * components : 4 * components]
                flow_sum, adjoint_sum, tang_sum, second_sum = (
                    functools.reduce(lambda a, b: a + b, part)
                    for part in (flow, adjoint, tang, second)
                )
                for c in range(components):
                    rows[step, c, at, lanes] = flow[c] * tang_sum + tang[c] * flow_sum
                    rows[step, components + c, at, lanes] = (
                        flow[c] * second_sum
                        + second[c] * flow_sum
                        + adjoint[c] * tang_sum
                        + tang[c] * adjoint_sum
                    )
            return carry

        lax.fori_loop(0, middle // 8, each, 0)

    barrier = pltpu.get_barrier_semaphore()

    def greet_az(hop, carry):
        pl.semaphore_signal(
            barrier, inc=1, device_id={"az": (my_az + hop) % az}, device_id_type=MESH
        )
        return carry

    def greet_ax(hop, carry):
        pl.semaphore_signal(
            barrier, inc=1, device_id={"ax": (my_ax + hop) % ax}, device_id_type=MESH
        )
        return carry

    lax.fori_loop(1, az, greet_az, 0)
    lax.fori_loop(1, ax, greet_ax, 0)
    pl.semaphore_wait(barrier, az + ax - 2)

    for step in range(min(lookahead, steps)):
        start(az, copy_in, own_in, step)

    def turn(now, carry):
        @pl.when(now < steps)
        def _():
            arrive(az, copy_in, own_in, now)

            @pl.when(now + lookahead < steps)
            def _():
                start(az, copy_in, own_in, now + lookahead)

            along_azimuth(now, fields)
            start(ax, copy_over, own_over, now)

        @pl.when((now >= 1) & (now < steps + 1))
        def _():
            step = now - 1
            arrive(ax, copy_over, own_over, step)
            along_axial(step, fields)
            multiply(step)
            along_axial(step, produced)
            start(ax, copy_back, own_back, step)

        @pl.when(now >= 2)
        def _():
            step = now - 2
            leave(ax, copy_over, step)
            arrive(ax, copy_back, own_back, step)
            fetch = pltpu.make_async_copy(
                back_ref.at[step], columns.at[step, pl.ds(0, produced)], own.at[4, step]
            )
            fetch.start()
            fetch.wait()
            along_azimuth(step, produced)
            start(az, copy_out, own_out, step)

        return carry

    lax.fori_loop(0, steps + 2, turn, 0)

    def finish(step, carry):
        arrive(az, copy_out, own_out, step)
        leave(az, copy_in, step)
        leave(ax, copy_back, step)
        leave(az, copy_out, step)
        return carry

    lax.fori_loop(0, steps, finish, 0)


def exchange(grid, az, ax):
    radial_count, fields, local_azimuth, local_axial = grid.shape
    azimuth_count = local_azimuth * az
    axial_count = local_axial * ax
    steps = radial_count // az
    produced = fields // 2
    middle = azimuth_count // ax
    columns = (steps, fields, azimuth_count, local_axial)
    rows = (steps, fields, middle, axial_count)
    group_rows = produced * middle
    points = radial_count * fields * azimuth_count * axial_count // (az * ax)
    semaphores = lambda count: pltpu.SemaphoreType.DMA((steps, count - 1))
    return pl.pallas_call(
        functools.partial(kernel, az, ax),
        out_shape=[
            jax.ShapeDtypeStruct(
                (radial_count, produced, local_azimuth, local_axial), jnp.float32
            ),
            jax.ShapeDtypeStruct((steps, produced, azimuth_count, local_axial), jnp.float32),
        ],
        in_specs=[
            pl.BlockSpec(memory_space=pl.ANY),
            pl.BlockSpec(memory_space=pltpu.VMEM),
            pl.BlockSpec(memory_space=pltpu.VMEM),
        ],
        out_specs=[pl.BlockSpec(memory_space=pl.ANY)] * 2,
        scratch_shapes=[
            pltpu.VMEM(columns, jnp.float32),
            pltpu.VMEM(rows, jnp.float32),
            pltpu.VMEM((group_rows, axial_count), jnp.bfloat16),
            pltpu.VMEM((group_rows, axial_count), jnp.bfloat16),
            semaphores(az),
            semaphores(az),
            semaphores(ax),
            semaphores(ax),
            semaphores(ax),
            semaphores(ax),
            semaphores(az),
            semaphores(az),
            pltpu.SemaphoreType.DMA((5, steps)),
        ],
        compiler_params=pltpu.CompilerParams(
            collective_id=0, has_side_effects=True, vmem_limit_bytes=60 * 2**20
        ),
        cost_estimate=pl.CostEstimate(
            flops=9 * points * (azimuth_count + axial_count),
            bytes_accessed=8 * points,
            transcendentals=0,
        ),
        name="exchange",
    )(grid, halves(hartley_table(azimuth_count)), halves(hartley_table(axial_count)))[0]


def dot_split(table_ref, value):
    high, low = split(value)
    return dot(table_ref[0], high) + (dot(table_ref[1], high) + dot(table_ref[0], low))


def to_grid_kernel(table_ref, flow_ref, adjoint_ref, tangent_ref, second_ref, out_ref):
    _, rows, radial_count, lanes = flow_ref.shape
    for field, ref in enumerate((flow_ref, adjoint_ref, tangent_ref, second_ref)):
        value = dot_split(table_ref, ref[0].reshape(rows * radial_count, lanes))
        out_ref[:, field, 0] = value.reshape(radial_count, rows, lanes)


def to_grid(table, fields):
    components, local_azimuth, radial_count, local_axial = fields[0].shape
    count = len(fields)
    out = pl.pallas_call(
        to_grid_kernel,
        grid=(local_azimuth // 8, components),
        out_shape=jax.ShapeDtypeStruct(
            (radial_count, count, components, local_azimuth, local_axial), jnp.float32
        ),
        in_specs=[pl.BlockSpec(table.shape, lambda m, c: (0, 0, 0))]
        + [pl.BlockSpec((1, 8, radial_count, local_axial), lambda m, c: (c, m, 0, 0))] * count,
        out_specs=pl.BlockSpec(
            (radial_count, count, 1, 8, local_axial), lambda m, c: (0, 0, c, m, 0)
        ),
        compiler_params=pltpu.CompilerParams(vmem_limit_bytes=40 * 2**20),
        name="to_grid",
    )(table, *fields)
    return out.reshape(radial_count, count * components, local_azimuth, local_axial)


def from_grid_kernel(
    table_ref, turned_ref, tangent_ref, second_ref, rate_ref, axial_ref, next_ref, after_ref
):
    _, rows, radial_count, lanes = tangent_ref.shape
    denom = 1.0 + viscosity * (rate_ref[...] + axial_ref[...].reshape(1, 1, lanes))
    for field, (ref, out_ref) in enumerate(((tangent_ref, next_ref), (second_ref, after_ref))):
        value = turned_ref[:, field, 0].reshape(radial_count * rows, lanes)
        term = dot_split(table_ref, value).reshape(rows, radial_count, lanes)
        out_ref[0] = (ref[0] + time_step * term) / denom


def from_grid(table, turned, tangent, second_adjoint, rate, axial):
    components, local_azimuth, radial_count, local_axial = tangent.shape
    turned = turned.reshape(radial_count, 2, components, local_azimuth, local_axial)
    spectral = pl.BlockSpec((1, 8, radial_count, local_axial), lambda m, c: (c, m, 0, 0))
    return pl.pallas_call(
        from_grid_kernel,
        grid=(local_azimuth // 8, components),
        out_shape=[jax.ShapeDtypeStruct(tangent.shape, jnp.float32)] * 2,
        in_specs=[
            pl.BlockSpec(table.shape, lambda m, c: (0, 0, 0)),
            pl.BlockSpec((radial_count, 2, 1, 8, local_axial), lambda m, c: (0, 0, c, m, 0)),
            spectral,
            spectral,
            pl.BlockSpec((8, radial_count, 1), lambda m, c: (m, 0, 0)),
            pl.BlockSpec((1, local_axial), lambda m, c: (0, 0)),
        ],
        out_specs=[spectral] * 2,
        compiler_params=pltpu.CompilerParams(vmem_limit_bytes=40 * 2**20),
        name="from_grid",
    )(table, turned, tangent, second_adjoint, rate, axial)


def body(saved_flow, saved_adjoint, tangent, second_adjoint, radial_rate):
    local_azimuth = tangent.shape[1]
    radial_count = tangent.shape[2]
    local_axial = tangent.shape[3]
    az = lax.axis_size("az")
    ax = lax.axis_size("ax")
    azimuth_count = local_azimuth * az
    axial_count = local_axial * ax
    table = np.einsum("jr,mn->jmnr", radial_table(radial_count), np.eye(8))
    table = table.reshape(8 * radial_count, 8 * radial_count)
    grid = to_grid(halves(table), (saved_flow, saved_adjoint, tangent, second_adjoint))
    turned = exchange(grid, az, ax)
    azimuth = lax.axis_index("az") * local_azimuth + jnp.arange(local_azimuth, dtype=jnp.int32)
    wave_azimuth = jnp.minimum(azimuth, azimuth_count - azimuth).astype(jnp.float32)
    axial = lax.axis_index("ax") * local_axial + jnp.arange(local_axial, dtype=jnp.int32)
    wave_axial = jnp.minimum(axial, axial_count - axial).astype(jnp.float32) * axial_unit
    rate = radial_rate[None, :, None] + (wave_azimuth**2)[:, None, None]
    return tuple(
        from_grid(
            halves(table.T), turned, tangent, second_adjoint, rate, (wave_axial**2)[None, :]
        )
    )


def solution(mesh):
    in_specs = (
        P(None, "az", None, "ax"),
        P(None, "az", None, "ax"),
        P(None, "az", None, "ax"),
        P(None, "az", None, "ax"),
        P(),
    )
    out_specs = (P(None, "az", None, "ax"), P(None, "az", None, "ax"))
    return jax.shard_map(body, mesh=mesh, in_specs=in_specs, out_specs=out_specs, check_vma=False)
```

time: 1850 us -> 876 us (0.47)
  Pallas kernels: 0 us -> 855 us
  blocking collectives: 697 us -> 0 us
  waiting for transfers between devices: 528 us -> 0 us
  matrix products: 276 us -> 0 us
  local copies, waits for them, and re-layouts: 223 us -> 9.57 us
  other arithmetic: 106 us -> 0.22 us
    pallas_call x0 -> x3, Pallas kernels: none -> 855 us  [the longest x1 811 us: exchange(): pl.pallas_call(functools.partial(kernel, az, ax), out_shape=[jax.ShapeDty...]
    all_to_all x2 -> x0, blocking collectives: 697 us -> none  [the longest x1 551 us: body(): lax.all_to_all(grid, 'az', split_axis=2, concat_axis=1, tiled=True)]
    all_to_all x2 -> x0, waiting for transfers between devices: 528 us -> none  [the longest x1 273 us: body(): lax.all_to_all(turned, 'az', split_axis=1, concat_axis=2, tiled=True)]
    dot_general x6 -> x0, matrix products: 276 us -> none  [the longest x2 148 us: along_axial(): jnp.einsum('nk,cmjk->cmjn', axial_table, field, precision=lax.Precision.H...]
    all_to_all x5 -> x0, local copies, waits for them, and re-layouts: 75.8 us -> none  [the longest x3 37.1 us: body(): lax.all_to_all(partial_field, 'ax', split_axis=3, concat_axis=1, tiled=True)]
    transpose x3 -> x0, local copies, waits for them, and re-layouts: 59.7 us -> none  [the longest x2 37.9 us: along_azimuth(): jnp.einsum('nm,cmjk->cnjk', azimuth_table, field, precision=lax.Precision...]
    unnamed x12, local copies, waits for them, and re-layouts: 65.7 us -> 9.57 us
    all_to_all x1 -> x0, other arithmetic: 39.8 us -> none  [body(): lax.all_to_all(partial_field, 'ax', split_axis=3, concat_axis=1, tiled=True)]
  transfers between devices with their start and end apart: 2 -> 0, of which waited for: 2 -> 0; matrix products, arithmetic and copies ran while one was open for 1% -> 0% of each run, Pallas kernels for 0% -> 0%
where the time goes in v1:
time: 876 us; the launch traced here: 865 us
  Pallas kernels  855 us (98%)
  local copies, waits for them, and re-layouts  9.57 us (1%)
    pallas_call x1, Pallas kernels, exchange(): pl.pallas_call(functools.partial(kernel, az, ax), out_shape=[jax.ShapeDty...  811 us
    pallas_call x1, Pallas kernels, to_grid(): pl.pallas_call(to_grid_kernel, grid=(local_azimuth // 8, components), out...  25.3 us
    pallas_call x1, Pallas kernels, from_grid(): pl.pallas_call(from_grid_kernel, grid=(local_azimuth // 8, components), o...  18.8 us

profile of v1, /device:TPU:0, one launch (start us, length us, event | category | flops | bytes accessed | tf_op | source)
XLA Modules:
  0.0 865.3 jit_solution(8330470071684696419)
XLA Ops:
  0.6 0.0 copy-start.1
  0.6 2.8 copy-done.1
  3.4 0.0 copy-start.2
  3.4 2.8 copy-done.2
  6.2 0.0 copy-start.3
  6.2 1.2 copy-done.3
  7.4 25.3 %to_grid.1 = f32[64,4,3,32,256]{4,3,2,1,0:T(8,128)} custom-call(bf16[2,512,512]{2,1,0:T(8,128)(2,1)S(1)} %copy-done.3, f32[3,32,64,256]{3,2,1,0:T(8,128)S(1)} %copy-done.1, f32[3,32,64,256]{3,2,1,0:T(8,128)S(1)} %copy-done.2, f32[3,32,64,256]{3,2,1,0:T(8,128)} %tangent_ref.3, f32[3,32,64,256]{3,2,1,0:T(8,128)} %second_ref.3), custom_call_target="tpu_custom_call" | custom-call | tf_op jit(solution)/shard_map/to_grid/pallas_call | solution.py:391
  32.7 0.0 copy-start.5
  32.7 0.0 copy-start.4
  32.7 810.7 %exchange.1 = (f32[64,6,32,256]{3,2,1,0:T(8,128)}, f32[8,6,256,256]{3,2,1,0:T(8,128)}) custom-call(f32[64,12,32,256]{3,2,1,0:T(8,128)} %bitcast.2, bf16[2,256,256]{2,1,0:T(8,128)(2,1)} %constant.26.clone.azimuth_ref, bf16[2,1024,1024]{2,1,0:T(8,128)(2,1)} %constant.27.clone.axial_ref), custom_call_target="tpu_custom_call" | custom-call | flops 72477573120 | bytes 50331648 | tf_op jit(solution)/shard_map/exchange/pallas_call | solution.py:335
  843.4 0.0 copy-done.5
  843.4 0.2 broadcast_add_fusion.rate_ref
  843.7 0.0 copy-done.4
  843.7 0.0 copy-start
  843.7 2.8 copy-done
  846.5 18.8 %from_grid.1 = (f32[3,32,64,256]{3,2,1,0:T(8,128)}, f32[3,32,64,256]{3,2,1,0:T(8,128)}) custom-call(bf16[2,512,512]{2,1,0:T(8,128)(2,1)S(1)} %copy-done.4, f32[64,2,3,32,256]{4,3,2,1,0:T(8,128)} %bitcast.3, f32[3,32,64,256]{3,2,1,0:T(8,128)S(1)} %copy-done, f32[3,32,64,256]{3,2,1,0:T(8,128)} %second_ref.3, f32[32,64,1]{2,1,0:T(8,128)S(1)} %broadcast_add_fusion.rate_ref, ...), custom_call_target="tpu_custom_call" | custom-call | tf_op jit(solution)/shard_map/from_grid/pallas_call | solution.py:423
  (2 shorter events, 0.0 us)
Async XLA Ops:
  0.6 2.8 copy-start.1
  3.4 2.8 copy-start.2
  6.2 1.2 copy-start.3
  32.7 810.7 %copy-start.5 = (f32[64]{0:T(128)S(1)}, f32[64]{0:T(128)}, u32[]{:S(2)}) copy-start(f32[64]{0:T(128)} %param.13) | copy-start | bytes 772
  32.7 811.0 %copy-start.4 = (bf16[2,512,512]{2,1,0:T(8,128)(2,1)S(1)}, bf16[2,512,512]{2,1,0:T(8,128)(2,1)}, u32[]{:S(2)}) copy-start(bf16[2,512,512]{2,1,0:T(8,128)(2,1)} %constant.28.clone.table_ref) | copy-start | bytes 3145732
  843.7 2.8 copy-start
